TPU v7x, 32 devices: a whole 2x2x4 slice. The times are simulated.
32 devices in a mesh: center: 8 (over z, x), batch: 4 (over y, core).
Axes of the slice: x: 2, y: 2, z: 4, core: 2. Of those that a mesh axis runs over, the one named last changes fastest.
Arguments:
- centers: bfloat16 [4096, 384], P('center'), may hold values from -4 to 4
- weights: bfloat16 [4096, 512], P('center'), may hold values from -1 to 1
- subset_index: int32 [768], P('center'), may hold values from 0 to 4095, as said below
- basis: bfloat16 [768, 256], P('center'), may hold values from -2 to 2
- damping: float32 [256], replicated, may hold values from 0.2 to 0.95
- stored_train_features: bfloat16 [4, 512, 384], P('batch', 'center'), may hold values from -4 to 4
- pool_labels: bfloat16 [4, 512, 512], P('batch', 'center'), may hold values from -4 to 4
- picks: int32 [4, 16], P('batch', 'center'), may hold values from 0 to 63
Outputs:
- new_weights: bfloat16 [4096, 512], P('center')
- residual: bfloat16 [4, 16, 512], P('batch', 'center')
Inputs may be any that keep to these rules, and one draw needn't show every extreme that they name: `subset_index`: the entries are distinct centers; center p is held by index p // 512 of center. Of the 96 entries on one device at most 48 are held by any one index, and in every draw some index holds exactly 48 of the entries of every device.
All inputs are finite; a program needn't handle non-finite values.
Results may differ from a plain program's by a relative error of at most 0.013.
Values may be sent and summed in bfloat16 or wider, within the bound.
A program may use at most 64 MiB of HBM per device.

v0:
```python
import jax
import jax.numpy as jnp
from jax import lax
from jax.sharding import PartitionSpec as P

kernel_length = 2.0
step_rate = 0.1


def per_device(
    centers, weights, subset_index, basis, damping, stored_train_features, pool_labels, picks
):
    devices = lax.axis_size("center")
    own_rows = picks.shape[1]
    center_rows = centers.shape[0]
    own_features = jnp.take(stored_train_features[0], picks[0], axis=0)
    own_targets = jnp.take(pool_labels[0], picks[0], axis=0)
    centers_sq = jnp.sum(jnp.square(centers.astype(jnp.float32)), axis=1)
    holder = subset_index // center_rows
    local_row = subset_index - holder * center_rows
    entries = subset_index.shape[0]
    capacity = 4 * entries // devices
    same_holder = holder[:, None] == holder[None, :]
    earlier = (
        jnp.arange(entries, dtype=jnp.int32)[:, None]
        > jnp.arange(entries, dtype=jnp.int32)[None, :]
    )
    slot_rank = jnp.sum((same_holder & earlier).astype(jnp.int32), axis=1)
    send_rows = (
        jnp.zeros((devices, capacity, basis.shape[1]), jnp.bfloat16)
        .at[holder, slot_rank]
        .set(basis)
    )
    send_local = jnp.zeros((devices, capacity), jnp.int32).at[holder, slot_rank].set(local_row)
    got_rows, got_local = (
        lax.all_to_all(send_rows, "center", split_axis=0, concat_axis=0, tiled=True),
        lax.all_to_all(send_local, "center", split_axis=0, concat_axis=0, tiled=True),
    )
    flattened_row_list = got_rows.reshape(devices * capacity, basis.shape[1])
    flat_local = got_local.reshape(devices * capacity)
    group_features, group_targets = (
        lax.all_gather(own_features, "center", axis=0, tiled=True),
        lax.all_gather(own_targets, "center", axis=0, tiled=True),
    )
    portion_sq = jnp.sum(jnp.square(group_features.astype(jnp.float32)), axis=1)
    cross = lax.dot_general(
        group_features, centers, (((1,), (1,)), ((), ())), preferred_element_type=jnp.float32
    )
    distance = portion_sq[:, None] + centers_sq[None, :] - 2.0 * cross
    laplace_kernel = jnp.exp(-jnp.sqrt(jnp.maximum(distance, 0.0)) / kernel_length).astype(
        jnp.bfloat16
    )
    predicted = lax.psum(
        jnp.dot(laplace_kernel, weights, preferred_element_type=jnp.float32), "center"
    )
    group_residual = (predicted - group_targets.astype(jnp.float32)).astype(jnp.bfloat16)
    residual = lax.dynamic_slice_in_dim(
        group_residual, lax.axis_index("center") * own_rows, own_rows, 0
    )
    group_grad = lax.dot_general(
        laplace_kernel, group_residual, (((0,), (0,)), ((), ())), preferred_element_type=jnp.float32
    )
    gradient = step_rate * lax.psum(group_grad.astype(jnp.bfloat16), "batch").astype(jnp.float32)
    picked = jnp.take(gradient, flat_local, axis=0).astype(jnp.bfloat16)
    partial_projection = lax.dot_general(
        flattened_row_list, picked, (((0,), (0,)), ((), ())), preferred_element_type=jnp.float32
    )
    projected = lax.psum(partial_projection, "center")
    scaled = (damping[:, None] * projected).astype(jnp.bfloat16)
    correction = jnp.dot(flattened_row_list, scaled, preferred_element_type=jnp.float32)
    updated = (weights.astype(jnp.float32) - gradient).at[flat_local].add(correction)
    return (updated.astype(jnp.bfloat16), residual[None])


def solution(mesh):
    return jax.shard_map(
        per_device,
        mesh=mesh,
        in_specs=(
            P("center", None),
            P("center", None),
            P("center"),
            P("center", None),
            P(),
            P("batch", "center", None),
            P("batch", "center", None),
            P("batch", "center"),
        ),
        out_specs=(P("center", None), P("batch", "center", None)),
        check_vma=False,
    )
```

profile of v0, /device:TPU:0, one launch (start us, length us, event | category | flops | bytes accessed | tf_op | source)
XLA Modules:
  0.0 241.9 jit_solution(7291257038058377035)
XLA Ops:
  7.2 0.7 multiply_subtract_fusion
  7.9 0.2 convert_reduce_fusion
  8.1 0.6 broadcast_in_dim.57
  8.7 15.0 %scatter_fusion = s32[8,48]{1,0:T(8,128)} fusion(s32[8,48]{1,0:T(8,128)} %broadcast_in_dim.57, s32[96]{0:T(128)S(1)} %fusion.19, s32[96]{0:T(128)S(1)} %get-tuple-element.2), kind=kCustom, calls=%fused_computation.3 | custom fusion | bytes 1920 | tf_op jit(solution)/shard_map/scatter | solution.py:34
  23.7 7.4 %all-to-all-start = ((s32[8,1,48]{2,1,0:T(1,128)}), s32[8,1,48]{2,1,0:T(1,128)S(1)}, u32[]{:S(2)}, u32[]{:S(2)}) async-start(s32[8,1,48]{2,1,0:T(1,128)} %bitcast.11), calls=%async_computation | async-start | bytes 8192 | tf_op jit(solution)/shard_map/all_to_all | solution.py:37
  31.1 0.2 multiply_reduce_fusion
  31.3 1.4 gather_fusion
  32.7 0.6 gather_fusion.1
  33.4 26.4 %all-gather = bf16[8,2,384]{2,1,0:T(2,128)(2,1)S(1)} all-gather(bf16[1,2,384]{2,1,0:T(2,128)(2,1)S(1)} %fusion.15), channel_id=1, replica_groups=mesh['center'=8,'batch'=4] {'center'}, dimensions={0}, use_global_device_ids=true | all-gather | bytes 13824 | tf_op jit(solution)/shard_map/all_gather | solution.py:42
  59.8 0.1 multiply_reduce_fusion.1
  59.9 26.0 %all-gather.1 = bf16[8,2,512]{2,1,0:T(2,128)(2,1)S(1)} all-gather(bf16[1,2,512]{2,1,0:T(2,128)(2,1)S(1)} %fusion.13), channel_id=1, replica_groups=mesh['center'=8,'batch'=4] {'center'}, dimensions={0}, use_global_device_ids=true | all-gather | bytes 18432 | tf_op jit(solution)/shard_map/all_gather | solution.py:43
  86.0 0.2 fusion.6
  86.2 0.2 fusion.21
  86.4 34.1 %psum.21 = f32[16,512]{1,0:T(8,128)S(1)} all-reduce(f32[16,512]{1,0:T(8,128)S(1)} %fusion.21), channel_id=1, replica_groups=mesh['center'=8,'batch'=4] {'center'}, use_global_device_ids=true, to_apply=%region_2.3 | all-reduce | flops 8192 | bytes 65536 | tf_op jit(solution)/shard_map/psum | solution.py:53
  120.5 1.1 convolution_convert_fusion
  121.6 0.7 broadcast_in_dim.59
  122.3 0.1 copy-done.4
  122.4 11.7 %scatter_fusion.1 = bf16[8,48,256]{2,1,0:T(8,128)(2,1)} fusion(bf16[8,48,256]{2,1,0:T(8,128)(2,1)} %broadcast_in_dim.59, s32[96]{0:T(128)S(1)} %fusion.19, bf16[96,256]{1,0:T(8,128)(2,1)S(1)} %copy-done.4), kind=kCustom, calls=%fused_computation.4 | custom fusion | bytes 148224 | tf_op jit(solution)/shard_map/scatter | solution.py:32
  134.2 3.4 %all-to-all-start.1 = ((bf16[8,48,256]{2,1,0:T(8,128)(2,1)}), bf16[8,48,256]{2,1,0:T(8,128)(2,1)S(1)}, u32[]{:S(2)}, u32[]{:S(2)}) async-start(bf16[8,48,256]{2,1,0:T(8,128)(2,1)} %scatter_fusion.1), calls=%async_computation.1 | async-start | bytes 393216 | tf_op jit(solution)/shard_map/all_to_all | solution.py:36
  137.7 0.5 broadcast.167
  138.2 0.7 reduce.7
  139.0 13.2 %all-reduce.3.cloned.1.call-done = bf16[512,512]{1,0:T(8,128)(2,1)} async-done(((bf16[512,512]{1,0:T(8,128)(2,1)}), bf16[512,512]{1,0:T(8,128)(2,1)}) %all-reduce.3.cloned.1.call-update) | async-done | bytes 524304 | tf_op jit(solution)/shard_map/psum | solution.py:63
  152.3 1.1 convert_multiply_fusion
  153.4 2.1 gather_fusion.2
  155.5 1.2 fusion.7
  156.7 0.6 dynamic-slice_bitcast_fusion
  157.3 0.4 copy-done.2
  157.7 0.1 convert_subtract_fusion
  157.9 71.4 %all-reduce.5.cloned.1.call-done = f32[256,512]{1,0:T(8,128)} async-done(((f32[256,512]{1,0:T(8,128)}), f32[256,512]{1,0:T(8,128)}) %all-reduce.5.cloned.1.call-update) | async-done | bytes 524304 | tf_op jit(solution)/shard_map/psum | solution.py:68
  229.2 1.4 fusion.10
  230.6 3.5 %scatter_fusion.2 = f32[512,512]{1,0:T(8,128)S(1)} fusion(f32[512,512]{1,0:T(8,128)S(1)} %convert_subtract_fusion, s32[384]{0:T(512)S(1)} %fusion.14, f32[384,512]{1,0:T(8,128)S(1)} %fusion.10), kind=kCustom, calls=%fused_computation.5 | custom fusion | flops 196608 | bytes 2360832 | tf_op jit(solution)/shard_map/scatter-add | solution.py:71
  234.2 0.9 convert_element_type.47
  (32 shorter events, 0.6 us)
Async XLA Ops:
  7.2 25.5 %copy-start = (bf16[1,64,512]{2,1,0:T(8,128)(2,1)S(1)}, bf16[1,64,512]{2,1,0:T(8,128)(2,1)}, u32[]{:S(2)}) copy-start(bf16[1,64,512]{2,1,0:T(8,128)(2,1)} %param.14) | copy-start | bytes 196612
  8.7 22.4 %copy-start.6 = (s32[1,2]{1,0:T(1,128)S(1)}, s32[1,2]{1,0:T(1,128)}, u32[]{:S(2)}) copy-start(s32[1,2]{1,0:T(1,128)} %param.15) | copy-start | bytes 28
  8.7 22.5 %copy-start.3 = (bf16[512,384]{1,0:T(8,128)(2,1)S(1)}, bf16[512,384]{1,0:T(8,128)(2,1)}, u32[]{:S(2)}) copy-start(bf16[512,384]{1,0:T(8,128)(2,1)} %param.8) | copy-start | bytes 1179652
  23.7 62.5 %copy-start.1 = (bf16[512,512]{1,0:T(8,128)(2,1)S(1)}, bf16[512,512]{1,0:T(8,128)(2,1)}, u32[]{:S(2)}) copy-start(bf16[512,512]{1,0:T(8,128)(2,1)} %param.9) | copy-start | bytes 1572868
  23.7 110.5 %all-to-all-start = ((s32[8,1,48]{2,1,0:T(1,128)}), s32[8,1,48]{2,1,0:T(1,128)S(1)}, u32[]{:S(2)}, u32[]{:S(2)}) async-start(s32[8,1,48]{2,1,0:T(1,128)} %bitcast.11), calls=%async_computation | async-start | bytes 8192 | tf_op jit(solution)/shard_map/all_to_all | solution.py:37
  31.0 121.2 %all-reduce.3.cloned.1.call-start = ((), (), s32[]{:S(2)}) async-start(), calls=%async_computation.2 | async-start | bytes 1048576 | tf_op jit(solution)/shard_map/psum | solution.py:63
  121.6 0.8 copy-start.4
  134.2 21.3 %all-to-all-start.1 = ((bf16[8,48,256]{2,1,0:T(8,128)(2,1)}), bf16[8,48,256]{2,1,0:T(8,128)(2,1)S(1)}, u32[]{:S(2)}, u32[]{:S(2)}) async-start(bf16[8,48,256]{2,1,0:T(8,128)(2,1)} %scatter_fusion.1), calls=%async_computation.1 | async-start | bytes 393216 | tf_op jit(solution)/shard_map/all_to_all | solution.py:36
  137.6 91.7 %all-reduce.5.cloned.1.call-start = ((), (), s32[]{:S(2)}) async-start(), calls=%async_computation.3 | async-start | bytes 1048576 | tf_op jit(solution)/shard_map/psum | solution.py:68
  156.7 1.0 copy-start.2
  157.7 71.5 %copy-start.5 = (f32[256]{0:T(256)S(1)}, f32[256]{0:T(256)}, u32[]{:S(2)}) copy-start(f32[256]{0:T(256)} %param.12) | copy-start | bytes 3076
Sparse Core Ops, SparseCore 0:
  121.7 30.4 all-reduce.2
  156.8 72.3 all-reduce.4
where the time goes:
time: 243 us; the launch traced here: 242 us
  blocking collectives  86.5 us (36%)
  waiting for transfers between devices  84.7 us (35%)
  local copies, waits for them, and re-layouts  33.9 us (14%)
  between operations  14.2 us (6%)
  starting transfers between devices  10.9 us (4%)
  other arithmetic  7.7 us (3%)
  matrix products  4.07 us (2%)
    psum x1, waiting for transfers between devices, per_device(): projected = lax.psum(partial_projection, 'center')  71.4 us
    psum x1, blocking collectives, per_device(): lax.psum(jnp.dot(laplace_kernel, weights, preferred_element_type=jnp.floa...  34.1 us
    all_gather x1, blocking collectives, per_device(): lax.all_gather(own_features, 'center', axis=0, tiled=True)  26.4 us
    all_gather x1, blocking collectives, per_device(): lax.all_gather(own_targets, 'center', axis=0, tiled=True)  26 us
    scatter x1, local copies, waits for them, and re-layouts, per_device(): jnp.zeros((devices, capacity), jnp.int32).at[holder, slot_rank]  15 us
    psum x1, waiting for transfers between devices, per_device(): lax.psum(group_grad.astype(jnp.bfloat16), 'batch').astype(jnp.float32)  13.2 us
    scatter x1, local copies, waits for them, and re-layouts, per_device(): send_rows = jnp.zeros((devices, capacity, basis.shape[1]), jnp.bfloat16)....  11.7 us
    all_to_all x1, starting transfers between devices, per_device(): lax.all_to_all(send_local, 'center', split_axis=0, concat_axis=0, tiled=T...  7.38 us
  transfers between devices with their start and end apart: 4, of which 2 were waited for; matrix products, arithmetic and copies ran while one was open for 9% of the time, Pallas kernels for 0%

commit v1 on v0

v1 whole, which is shorter than its diff:
```python
import functools

import jax
import jax.numpy as jnp
from jax import lax
from jax.experimental import pallas as pl
from jax.experimental.pallas import tpu as pltpu
from jax.sharding import PartitionSpec as P

MESH = pl.DeviceIdType.MESH
kernel_length = 2.0
step_rate = 0.1
LANES = 128
F32, BF16 = jnp.float32, jnp.bfloat16


def dot(a, b, ca=1, cb=0):
    return lax.dot_general(a, b, (((ca,), (cb,)), ((), ())), preferred_element_type=F32)


def each(count, body):
    if count <= 8:
        for k in range(count):
            body(k)
    else:
        lax.fori_loop(0, count, lambda k, c: (body(k), c)[1], 0)


def round_up(x, m):
    return (x + m - 1) // m * m


def laplace(features, sq_centers, center_rows):
    wide = features.astype(F32)
    sq_samples = jnp.sum(wide * wide, axis=1, keepdims=True)
    distance = sq_samples + sq_centers - 2.0 * dot(features, center_rows, 1, 1)
    return jnp.exp(-jnp.sqrt(jnp.maximum(distance, 0.0)) / kernel_length)


def step_kernel(
    n, nb, rank_rows, slot_rows,
    centers_h, weights_h, idx_ref, basis_h, damping_ref, pool_h, labels_h, picks_ref,
    out_w, out_r,
    centers, weights, basis, pool, labels, idx_row,
    feat, feat_f32, feat_all, pack_out, pack_in, place_out, place_in,
    sums_out, sums_in, back, back_f32, back_all,
    local_sem, send_sem, recv_sem,
):
    me, mb = lax.axis_index("center"), lax.axis_index("batch")
    own, D = feat.shape[1:]
    PC, C = weights.shape
    S, Q = basis_h.shape
    SP = basis.shape[0]
    pool_rows = pool.shape[0]
    group = own * n

    loads = [
        pltpu.make_async_copy(src, dst, local_sem.at[i])
        for i, (src, dst) in enumerate(
            [
                (pool_h, pool),
                (basis_h, basis.at[pl.ds(0, S)]),
                (centers_h, centers),
                (labels_h, labels),
                (weights_h, weights),
            ]
        )
    ]
    for load in loads:
        load.start()
    pool_load, basis_load, centers_load, labels_load, weights_load = loads

    def center_peer(k):
        return lax.rem(me + 1 + k, n)

    def batch_peer(k):
        return lax.rem(mb + 1 + k, nb)

    barrier = pltpu.get_barrier_semaphore()

    def greet_center(k):
        pl.semaphore_signal(barrier, inc=1, device_id={"center": center_peer(k)}, device_id_type=MESH)

    def greet_batch(k):
        pl.semaphore_signal(barrier, inc=1, device_id={"batch": batch_peer(k)}, device_id_type=MESH)

    each(n - 1, greet_center)
    each(nb - 1, greet_batch)

    idx_row[...] = jnp.full(idx_row.shape, -1, jnp.int32)
    idx_row[:, 0:S] = idx_ref[...]
    if SP > S:
        basis[pl.ds(S, SP - S), :] = jnp.zeros((SP - S, Q), BF16)
    if slot_rows > rank_rows:
        pack_in[:, pl.ds(rank_rows, slot_rows - rank_rows), :] = jnp.zeros(
            (n, slot_rows - rank_rows, Q), BF16
        )
    idx = idx_row[...]
    nh = round_up(n, 16)
    first = lax.broadcasted_iota(jnp.int32, (nh, SP), 0) * PC
    inside = (idx >= first) & (idx < first + PC) & (first < n * PC)
    member = jnp.where(inside, 1.0, 0.0)
    before = jnp.where(
        lax.broadcasted_iota(jnp.int32, (SP, SP), 0) < lax.broadcasted_iota(jnp.int32, (SP, SP), 1), 1.0, 0.0
    )
    ranks = dot(member.astype(BF16), before.astype(BF16))
    rank = jnp.sum(member * ranks, axis=0, keepdims=True)
    holder = jnp.sum(
        member * lax.broadcasted_iota(jnp.int32, (nh, SP), 0).astype(F32), axis=0, keepdims=True
    )
    real = idx >= 0
    local = idx.astype(F32) - holder * PC
    packed_row = jnp.where(real, holder * rank_rows + rank, -1.0)
    share = LANES // slot_rows
    lane_start = (lax.rem(me, share) * slot_rows).astype(F32)
    code = jnp.where(real, holder * LANES + rank + lane_start, -1.0)
    code_t = jnp.transpose(jnp.broadcast_to(code, (LANES, SP)))
    local_t = jnp.transpose(jnp.broadcast_to(local, (LANES, SP))) + 1.0
    lane = lax.broadcasted_iota(jnp.int32, (SP, LANES), 1).astype(F32)

    def fill_place(h):
        hit = code_t == lane + lax.convert_element_type(h, F32) * LANES
        place_out[h] = jnp.sum(jnp.where(hit, local_t, 0.0), axis=0, keepdims=True)

    each(n, fill_place)
    chosen = lax.broadcasted_iota(jnp.int32, (n * rank_rows, SP), 0).astype(F32) == packed_row
    chosen = jnp.where(chosen, 1.0, 0.0).astype(BF16)

    pool_load.wait()
    lanes = lax.broadcasted_iota(jnp.int32, (8, pool_rows), 1)
    rows = lax.broadcasted_iota(jnp.int32, (8, pool_rows), 0)
    pick = jnp.zeros((8, pool_rows), jnp.bool_)
    for i in range(own):
        pick = pick | ((rows == i) & (lanes == picks_ref[0, i]))
    pick = jnp.where(pick, 1.0, 0.0).astype(BF16)
    feat[me] = dot(pick, pool[...])[0:own]

    basis_load.wait()
    pack_out[...] = dot(chosen, basis[...]).astype(BF16).reshape(n, rank_rows, Q)
    pack_in[me, pl.ds(0, rank_rows), :] = pack_out[me]
    place_in[me] = place_out[me]

    pl.semaphore_wait(barrier, n + nb - 2)

    def send(src, dst, i, device):
        pltpu.make_async_remote_copy(
            src_ref=src,
            dst_ref=dst,
            send_sem=send_sem.at[i],
            recv_sem=recv_sem.at[i],
            device_id=device,
            device_id_type=MESH,
        ).start()

    def finish(sem, i, ref):
        pltpu.make_async_copy(ref, ref, sem.at[i]).wait()

    rest = pl.ds(0, n - 1)
    rest_b = pl.ds(0, nb - 1)
    head = pl.ds(0, rank_rows)

    def send_feat(k):
        send(feat.at[me], feat.at[me], 0, {"center": center_peer(k)})

    def send_pack(k):
        j = center_peer(k)
        send(pack_out.at[j], pack_in.at[me, head], 1, {"center": j})
        send(place_out.at[j], place_in.at[me], 2, {"center": j})

    each(n - 1, send_feat)
    each(n - 1, send_pack)

    labels_load.wait()
    targets = dot(pick, labels[...])[0:own]
    centers_load.wait()
    center_rows = centers[...]
    wide = center_rows.astype(F32)
    square = wide * wide
    high = square.astype(BF16)
    low = (square - high.astype(F32)).astype(BF16)
    ones = jnp.ones((16, D), BF16)
    sq_centers = (dot(ones, high, 1, 1) + dot(ones, low, 1, 1))[0:1]

    finish(recv_sem, 0, feat.at[rest])
    for j in range(n):
        feat_f32[own * j : own * (j + 1), :] = feat[j]
    group_features = feat_f32[...].astype(BF16)
    feat_all[mb] = group_features
    kernel = laplace(group_features, sq_centers, center_rows).astype(BF16)
    weights_load.wait()
    predicted = dot(kernel, weights[...])

    finish(recv_sem, 1, pack_in.at[rest, head])
    finish(recv_sem, 2, place_in.at[rest])
    tiles = []
    for t in range(round_up(n, share) // share):
        row = place_in[t * share]
        for j in range(t * share + 1, min(n, (t + 1) * share)):
            row = row + place_in[j]
        centers_iota = (lax.broadcasted_iota(jnp.int32, (PC, LANES), 0) + 1).astype(F32)
        tiles.append(jnp.where(centers_iota == row, 1.0, 0.0).astype(BF16)[:, : min(n - t * share, share) * slot_rows])
    spread = jnp.concatenate(tiles, axis=1) if len(tiles) > 1 else tiles[0]
    own_basis = dot(spread, pack_in[...].reshape(n * slot_rows, Q)).astype(BF16)
    overlap = dot(kernel, own_basis)

    for j in range(n):
        sums_out[j, :, 0:C] = predicted[own * j : own * (j + 1)]
        sums_out[j, :, C : C + Q] = overlap[own * j : own * (j + 1)]
    sums_in[me] = sums_out[me]

    def send_sums(k):
        j = center_peer(k)
        send(sums_out.at[j], sums_in.at[me], 3, {"center": j})

    def send_group(k):
        send(feat_all.at[mb], feat_all.at[mb], 4, {"batch": batch_peer(k)})

    each(n - 1, send_sums)
    each(nb - 1, send_group)

    finish(recv_sem, 3, sums_in.at[rest])
    total = jnp.sum(sums_in[...], axis=0)
    residual = (total[:, 0:C] - targets).astype(BF16)
    out_r[...] = residual
    back[me, :, 0:C] = residual.astype(F32)
    back[me, :, C : C + Q] = total[:, C:] * damping_ref[...] * step_rate

    def send_back(k):
        send(back.at[me], back.at[me], 5, {"center": center_peer(k)})

    each(n - 1, send_back)

    finish(recv_sem, 4, feat_all.at[rest_b])
    all_features = feat_all[...].reshape(nb * group, D)
    kernel_t = jnp.transpose(laplace(all_features, sq_centers, center_rows)).astype(BF16)

    finish(recv_sem, 5, back.at[rest])
    for j in range(n):
        back_f32[own * j : own * (j + 1), :] = back[j]
    overlap_f32 = back_f32[:, C : C + Q]
    overlap_high = overlap_f32.astype(BF16)
    back_all[mb, :, 0:C] = back_f32[:, 0:C].astype(BF16)
    back_all[mb, :, C : C + Q] = overlap_high
    back_all[mb, :, C + Q : C + 2 * Q] = (overlap_f32 - overlap_high.astype(F32)).astype(BF16)

    def send_back_batch(k):
        send(back_all.at[mb], back_all.at[mb], 6, {"batch": batch_peer(k)})

    each(nb - 1, send_back_batch)
    finish(recv_sem, 6, back_all.at[rest_b])

    everything = back_all[...].reshape(nb * group, C + 2 * Q)
    residuals = everything[:, 0:C]
    scaled = dot(everything[:, C : C + Q], residuals, 0, 0) + dot(everything[:, C + Q :], residuals, 0, 0)
    correction = dot(own_basis, scaled.astype(BF16))
    gradient = step_rate * dot(kernel_t, residuals)
    out_w[...] = ((weights[...].astype(F32) - gradient) + correction).astype(BF16)

    finish(send_sem, 0, feat.at[rest])
    finish(send_sem, 1, pack_in.at[rest, head])
    finish(send_sem, 2, place_in.at[rest])
    finish(send_sem, 3, sums_in.at[rest])
    finish(send_sem, 4, feat_all.at[rest_b])
    finish(send_sem, 5, back.at[rest])
    finish(send_sem, 6, back_all.at[rest_b])


def solution(mesh):
    n, nb = mesh.shape["center"], mesh.shape["batch"]

    def per_device(centers, weights, subset_index, basis, damping, stored, labels, picks):
        (PC, D), C = centers.shape, weights.shape[1]
        S, Q = basis.shape
        SP = round_up(S, LANES)
        own, pool_rows = picks.shape[1], stored.shape[1]
        group = own * n
        capacity = max(1, 4 * S // n)
        rank_rows = round_up(capacity, 16)
        slot_rows = 16
        while slot_rows < rank_rows:
            slot_rows *= 2
        anywhere = pl.BlockSpec(memory_space=pl.ANY)
        vmem = pl.BlockSpec(memory_space=pltpu.VMEM)
        smem = pl.BlockSpec(memory_space=pltpu.SMEM)
        new_weights, residual = pl.pallas_call(
            functools.partial(step_kernel, n, nb, rank_rows, slot_rows),
            out_shape=(
                jax.ShapeDtypeStruct((PC, C), BF16),
                jax.ShapeDtypeStruct((own, C), BF16),
            ),
            in_specs=[anywhere, anywhere, vmem, anywhere, vmem, anywhere, anywhere, smem],
            out_specs=(vmem, vmem),
            scratch_shapes=[
                pltpu.VMEM((PC, D), BF16),
                pltpu.VMEM((PC, C), BF16),
                pltpu.VMEM((SP, Q), BF16),
                pltpu.VMEM((pool_rows, D), BF16),
                pltpu.VMEM((pool_rows, C), BF16),
                pltpu.VMEM((1, SP), jnp.int32),
                pltpu.VMEM((n, own, D), F32),
                pltpu.VMEM((group, D), F32),
                pltpu.VMEM((nb, group, D), BF16),
                pltpu.VMEM((n, rank_rows, Q), BF16),
                pltpu.VMEM((n, slot_rows, Q), BF16),
                pltpu.VMEM((n, 1, LANES), F32),
                pltpu.VMEM((n, 1, LANES), F32),
                pltpu.VMEM((n, own, C + Q), F32),
                pltpu.VMEM((n, own, C + Q), F32),
                pltpu.VMEM((n, own, C + Q), F32),
                pltpu.VMEM((group, C + Q), F32),
                pltpu.VMEM((nb, group, C + 2 * Q), BF16),
                pltpu.SemaphoreType.DMA((5,)),
                pltpu.SemaphoreType.DMA((7,)),
                pltpu.SemaphoreType.DMA((7,)),
            ],
            compiler_params=pltpu.CompilerParams(
                collective_id=0, has_side_effects=True, vmem_limit_bytes=40 * 1024 * 1024
            ),
        )(
            centers,
            weights,
            subset_index.reshape(1, S),
            basis,
            damping.reshape(1, Q),
            stored[0],
            labels[0],
            picks,
        )
        return new_weights, residual[None]

    return jax.shard_map(
        per_device,
        mesh=mesh,
        in_specs=(
            P("center", None),
            P("center", None),
            P("center"),
            P("center", None),
            P(),
            P("batch", "center", None),
            P("batch", "center", None),
            P("batch", "center"),
        ),
        out_specs=(P("center", None), P("batch", "center", None)),
        check_vma=False,
    )
```

time: 243 us -> 33 us (0.14)
  blocking collectives: 86.5 us -> 0 us
  waiting for transfers between devices: 84.7 us -> 0 us
  local copies, waits for them, and re-layouts: 33.9 us -> 6.52 us
  Pallas kernels: 0 us -> 25.4 us
  between operations: 14.2 us -> 0.67 us
  starting transfers between devices: 10.9 us -> 0 us
  other arithmetic: 7.7 us -> 0 us
  matrix products: 4.07 us -> 0 us
    psum x2 -> x0, waiting for transfers between devices: 84.6 us -> none  [the longest x1 71.4 us: per_device(): projected = lax.psum(partial_projection, 'center')]
    all_gather x2 -> x0, blocking collectives: 52.4 us -> none  [the longest x1 26.4 us: per_device(): lax.all_gather(own_features, 'center', axis=0, tiled=True)]
    psum x1 -> x0, blocking collectives: 34.1 us -> none  [per_device(): lax.psum(jnp.dot(laplace_kernel, weights, preferred_element_type=jnp.floa...]
    scatter x2 -> x0, local copies, waits for them, and re-layouts: 26.7 us -> none  [the longest x1 15 us: per_device(): jnp.zeros((devices, capacity), jnp.int32).at[holder, slot_rank]]
    pallas_call x0 -> x1, Pallas kernels: none -> 25.4 us  [per_device(): pl.pallas_call(functools.partial(step_kernel, n, nb, rank_rows, slot_rows...]
    all_to_all x2 -> x0, starting transfers between devices: 10.8 us -> none  [the longest x1 7.38 us: per_device(): lax.all_to_all(send_local, 'center', split_axis=0, concat_axis=0, tiled=T...]
    unnamed x15 -> x18, local copies, waits for them, and re-layouts: 0.56 us -> 6.52 us
    dot_general x5 -> x0, matrix products: 4.07 us -> none  [the longest x1 1.36 us: per_device(): jnp.dot(flattened_row_list, scaled, preferred_element_type=jnp.float32)]
  transfers between devices with their start and end apart: 4 -> 0, of which waited for: 2 -> 0; matrix products, arithmetic and copies ran while one was open for 9% -> 0% of each run, Pallas kernels for 0% -> 0%
where the time goes in v1:
time: 33 us; the launch traced here: 32.6 us
  Pallas kernels  25.4 us (77%)
  local copies, waits for them, and re-layouts  6.52 us (20%)
  between operations  0.67 us (2%)
    pallas_call x1, Pallas kernels, per_device(): pl.pallas_call(functools.partial(step_kernel, n, nb, rank_rows, slot_rows...  25.4 us
    unnamed x18, local copies, waits for them, and re-layouts  6.52 us

profile of v1, /device:TPU:0, one launch (start us, length us, event | category | flops | bytes accessed | tf_op | source)
XLA Modules:
  0.0 32.6 jit_solution(10388835985475535950)
XLA Ops:
  0.6 0.0 copy-start.7
  0.6 0.0 copy-start.5
  0.7 0.0 copy-start.6
  0.7 0.6 %copy-done.7 = s32[1,2]{1,0:T(1,128)S(1)} copy-done((s32[1,2]{1,0:T(1,128)S(1)}, s32[1,2]{1,0:T(1,128)}, u32[]{:S(2)}) %copy-start.7) | copy-done | bytes 32
  1.3 0.0 copy-done.5
  1.3 0.0 copy-done.6
  1.3 0.0 copy-start
  1.3 1.0 %copy-done = bf16[512,512]{1,0:T(8,128)(2,1)S(1)} copy-done((bf16[512,512]{1,0:T(8,128)(2,1)S(1)}, bf16[512,512]{1,0:T(8,128)(2,1)}, u32[]{:S(2)}) %copy-start) | copy-done | bytes 524312
  2.4 0.0 copy-start.1
  2.4 1.0 %copy-done.1 = bf16[512,384]{1,0:T(8,128)(2,1)S(1)} copy-done((bf16[512,384]{1,0:T(8,128)(2,1)S(1)}, bf16[512,384]{1,0:T(8,128)(2,1)}, u32[]{:S(2)}) %copy-start.1) | copy-done | bytes 393240
  3.4 0.0 copy-start.2
  3.4 0.8 %copy-done.2 = bf16[1,64,512]{2,1,0:T(8,128)(2,1)S(1)} copy-done((bf16[1,64,512]{2,1,0:T(8,128)(2,1)S(1)}, bf16[1,64,512]{2,1,0:T(8,128)(2,1)}, u32[]{:S(2)}) %copy-start.2) | copy-done | bytes 65560
  4.2 0.0 copy-start.3
  4.2 0.8 %copy-done.3 = bf16[96,256]{1,0:T(8,128)(2,1)S(1)} copy-done((bf16[96,256]{1,0:T(8,128)(2,1)S(1)}, bf16[96,256]{1,0:T(8,128)(2,1)}, u32[]{:S(2)}) %copy-start.3) | copy-done | bytes 49176
  5.0 0.0 copy-start.4
  5.0 0.8 %copy-done.4 = bf16[1,64,384]{2,1,0:T(8,128)(2,1)S(1)} copy-done((bf16[1,64,384]{2,1,0:T(8,128)(2,1)S(1)}, bf16[1,64,384]{2,1,0:T(8,128)(2,1)}, u32[]{:S(2)}) %copy-start.4) | copy-done | bytes 49176
  5.8 25.4 %shard_map.95 = (bf16[512,512]{1,0:T(8,128)(2,1)S(1)}, bf16[2,512]{1,0:T(2,128)(2,1)S(1)}) custom-call(bf16[512,384]{1,0:T(8,128)(2,1)S(1)} %copy-done.1, bf16[512,512]{1,0:T(8,128)(2,1)S(1)} %copy-done, s32[1,96]{1,0:T(1,128)S(1)} %bitcast.9, bf16[96,256]{1,0:T(8,128)(2,1)S(1)} %copy-done.3, f32[1,256]{1,0:T(1,128)S(1)} %bitcast.8, ...), custom_call_target="tpu_custom_call" | custom-call | tf_op jit(solution)/shard_map/pallas_call | solution.py:285
  31.2 0.8 %copy.12 = bf16[512,512]{1,0:T(8,128)(2,1)} copy(bf16[512,512]{1,0:T(8,128)(2,1)S(1)} %get-tuple-element.8) | data formatting | bytes 1048576
  32.0 0.6 %copy.13 = bf16[1,2,512]{2,1,0:T(2,128)(2,1)} copy(bf16[1,2,512]{2,1,0:T(2,128)(2,1)S(1)} %bitcast.7) | data formatting | bytes 4096
Async XLA Ops:
  0.6 0.7 %copy-start.7 = (s32[1,2]{1,0:T(1,128)S(1)}, s32[1,2]{1,0:T(1,128)}, u32[]{:S(2)}) copy-start(s32[1,2]{1,0:T(1,128)} %picks_ref.1) | copy-start | bytes 28
  0.6 0.7 %copy-start.5 = (f32[256]{0:T(256)S(1)}, f32[256]{0:T(256)}, u32[]{:S(2)}) copy-start(f32[256]{0:T(256)} %param.12) | copy-start | bytes 3076
  0.7 0.7 %copy-start.6 = (s32[96]{0:T(128)S(1)}, s32[96]{0:T(128)}, u32[]{:S(2)}) copy-start(s32[96]{0:T(128)} %param.10) | copy-start | bytes 1156
  1.3 1.0 %copy-start = (bf16[512,512]{1,0:T(8,128)(2,1)S(1)}, bf16[512,512]{1,0:T(8,128)(2,1)}, u32[]{:S(2)}) copy-start(bf16[512,512]{1,0:T(8,128)(2,1)} %weights_h.1) | copy-start | bytes 1572868
  2.4 1.0 %copy-start.1 = (bf16[512,384]{1,0:T(8,128)(2,1)S(1)}, bf16[512,384]{1,0:T(8,128)(2,1)}, u32[]{:S(2)}) copy-start(bf16[512,384]{1,0:T(8,128)(2,1)} %centers_h.1) | copy-start | bytes 1179652
  3.4 0.8 %copy-start.2 = (bf16[1,64,512]{2,1,0:T(8,128)(2,1)S(1)}, bf16[1,64,512]{2,1,0:T(8,128)(2,1)}, u32[]{:S(2)}) copy-start(bf16[1,64,512]{2,1,0:T(8,128)(2,1)} %param.14) | copy-start | bytes 196612
  4.2 0.8 %copy-start.3 = (bf16[96,256]{1,0:T(8,128)(2,1)S(1)}, bf16[96,256]{1,0:T(8,128)(2,1)}, u32[]{:S(2)}) copy-start(bf16[96,256]{1,0:T(8,128)(2,1)} %basis_h.1) | copy-start | bytes 147460
  5.0 0.8 %copy-start.4 = (bf16[1,64,384]{2,1,0:T(8,128)(2,1)S(1)}, bf16[1,64,384]{2,1,0:T(8,128)(2,1)}, u32[]{:S(2)}) copy-start(bf16[1,64,384]{2,1,0:T(8,128)(2,1)} %param.13) | copy-start | bytes 147460

commit v2 on v1

v2 whole, which is shorter than its diff:
```python
import functools

import jax
import jax.numpy as jnp
from jax import lax
from jax.experimental import pallas as pl
from jax.experimental.pallas import tpu as pltpu
from jax.sharding import PartitionSpec as P

MESH = pl.DeviceIdType.MESH
kernel_length = 2.0
step_rate = 0.1
LANES = 128
F32, BF16 = jnp.float32, jnp.bfloat16


def dot(a, b, ca=1, cb=0):
    return lax.dot_general(a, b, (((ca,), (cb,)), ((), ())), preferred_element_type=F32)


def each(count, body):
    if count <= 8:
        for k in range(count):
            body(k)
    else:
        lax.fori_loop(0, count, lambda k, c: (body(k), c)[1], 0)


def round_up(x, m):
    return (x + m - 1) // m * m


def laplace(features, sq_centers, centers_t):
    wide = features.astype(F32)
    sq_samples = jnp.sum(wide * wide, axis=1, keepdims=True)
    distance = sq_samples + sq_centers - 2.0 * dot(features, centers_t)
    return jnp.exp(-jnp.sqrt(jnp.maximum(distance, 0.0)) / kernel_length)


def step_kernel(
    n, nb, rank_rows, slot_rows,
    centers_h, weights_h, idx_h, basis_h, damping_h, pool_h, labels_h, picks_h,
    out_w, out_r,
    centers, weights, basis, pool, labels, idx_ref, damping_ref, picks_ref, idx_row, centers_t,
    feat, feat_f32, feat_all, pack_out, pack_in, place_out, place_in,
    sums_out, sums_in, back, back_f32, back_all,
    local_sem, send_sem, recv_sem,
):
    me, mb = lax.axis_index("center"), lax.axis_index("batch")
    own, D = feat.shape[1:]
    PC, C = weights.shape
    S, Q = basis_h.shape
    SP = basis.shape[0]
    pool_rows = pool.shape[0]
    group = own * n

    loads = [
        pltpu.make_async_copy(src, dst, local_sem.at[i])
        for i, (src, dst) in enumerate(
            [
                (picks_h, picks_ref),
                (pool_h, pool),
                (idx_h, idx_ref),
                (basis_h, basis.at[pl.ds(0, S)]),
                (centers_h, centers),
                (weights_h, weights),
                (labels_h, labels),
                (damping_h, damping_ref),
            ]
        )
    ]
    for load in loads:
        load.start()
    (picks_load, pool_load, idx_load, basis_load, centers_load, weights_load, labels_load, damping_load) = loads

    def center_peer(k):
        return lax.rem(me + 1 + k, n)

    def batch_peer(k):
        return lax.rem(mb + 1 + k, nb)

    barrier = pltpu.get_barrier_semaphore()

    def greet_center(k):
        pl.semaphore_signal(barrier, inc=1, device_id={"center": center_peer(k)}, device_id_type=MESH)

    def greet_batch(k):
        pl.semaphore_signal(barrier, inc=1, device_id={"batch": batch_peer(k)}, device_id_type=MESH)

    each(n - 1, greet_center)
    each(nb - 1, greet_batch)

    idx_row[...] = jnp.full(idx_row.shape, -1, jnp.int32)
    if SP > S:
        basis[pl.ds(S, SP - S), :] = jnp.zeros((SP - S, Q), BF16)
    if slot_rows > rank_rows:
        pack_in[:, pl.ds(rank_rows, slot_rows - rank_rows), :] = jnp.zeros(
            (n, slot_rows - rank_rows, Q), BF16
        )

    def send(src, dst, i, device):
        pltpu.make_async_remote_copy(
            src_ref=src,
            dst_ref=dst,
            send_sem=send_sem.at[i],
            recv_sem=recv_sem.at[i],
            device_id=device,
            device_id_type=MESH,
        ).start()

    def finish(sem, i, ref):
        pltpu.make_async_copy(ref, ref, sem.at[i]).wait()

    rest = pl.ds(0, n - 1)
    rest_b = pl.ds(0, nb - 1)
    head = pl.ds(0, rank_rows)

    picks_load.wait()
    pool_load.wait()
    picks = picks_ref[...]
    lanes = lax.broadcasted_iota(jnp.int32, (8, pool_rows), 1)
    rows = lax.broadcasted_iota(jnp.int32, (8, pool_rows), 0)
    pick = jnp.zeros((8, pool_rows), F32)
    for i in range(own):
        pick = pick + jnp.where((rows == i) & (lanes == picks[:, i : i + 1]), 1.0, 0.0)
    pick = pick.astype(BF16)
    feat[me] = dot(pick, pool[...])[0:own]

    pl.semaphore_wait(barrier, n + nb - 2)

    def send_feat(k):
        send(feat.at[me], feat.at[me], 0, {"center": center_peer(k)})

    each(n - 1, send_feat)

    idx_load.wait()
    idx_row[:, 0:S] = idx_ref[...]
    idx = idx_row[...]
    nh = round_up(n, 16)
    holders = lax.broadcasted_iota(jnp.int32, (nh, SP), 0)
    first = holders * PC
    inside = (idx >= first) & (idx < first + PC) & (holders < n)
    member = jnp.where(inside, 1.0, 0.0)
    before = jnp.where(
        lax.broadcasted_iota(jnp.int32, (SP, SP), 0) < lax.broadcasted_iota(jnp.int32, (SP, SP), 1), 1.0, 0.0
    )
    ranks = dot(member.astype(BF16), before.astype(BF16))
    rank = jnp.sum(member * ranks, axis=0, keepdims=True)
    packed_row = jnp.sum(member * (ranks + holders.astype(F32) * rank_rows + 1.0), axis=0, keepdims=True)
    share = LANES // slot_rows
    lane = rank + (lax.rem(me, share) * slot_rows).astype(F32)
    at_lane = lax.broadcasted_iota(jnp.int32, (LANES, SP), 0).astype(F32) == lane
    at_lane = jnp.where(at_lane, 1.0, 0.0).astype(BF16)
    local = idx - first + 1
    parts = [jnp.where(inside, p.astype(F32), 0.0) for p in (local >> 8, local & 255)]
    places = dot(jnp.concatenate(parts, axis=0).astype(BF16), at_lane, 1, 1)
    places = 256.0 * places[0:nh] + places[nh:]
    for h in range(n):
        place_out[h] = places[h : h + 1]
    place_in[me] = place_out[me]

    def send_place(k):
        j = center_peer(k)
        send(place_out.at[j], place_in.at[me], 2, {"center": j})

    each(n - 1, send_place)

    chosen = (lax.broadcasted_iota(jnp.int32, (n * rank_rows, SP), 0) + 1).astype(F32) == packed_row
    chosen = jnp.where(chosen, 1.0, 0.0).astype(BF16)
    basis_load.wait()
    pack_out[...] = dot(chosen, basis[...]).astype(BF16).reshape(n, rank_rows, Q)

    def send_pack(k):
        j = center_peer(k)
        send(pack_out.at[j], pack_in.at[me, head], 1, {"center": j})

    each(n - 1, send_pack)
    pack_in[me, pl.ds(0, rank_rows), :] = pack_out[me]

    centers_load.wait()
    centers_t[...] = jnp.transpose(centers[...])
    wide = centers_t[...].astype(F32)
    sq_centers = jnp.sum(wide * wide, axis=0, keepdims=True)

    finish(recv_sem, 0, feat.at[rest])
    for j in range(n):
        feat_f32[own * j : own * (j + 1), :] = feat[j]
    group_features = feat_f32[...].astype(BF16)
    feat_all[mb] = group_features
    kernel = laplace(group_features, sq_centers, centers_t[...]).astype(BF16)
    weights_load.wait()
    predicted = dot(kernel, weights[...])

    finish(recv_sem, 2, place_in.at[rest])
    tiles = []
    for t in range(round_up(n, share) // share):
        row = place_in[t * share]
        for j in range(t * share + 1, min(n, (t + 1) * share)):
            row = row + place_in[j]
        local_row = (lax.broadcasted_iota(jnp.int32, (PC, LANES), 0) + 1).astype(F32)
        tile = jnp.where(local_row == row, 1.0, 0.0).astype(BF16)
        tiles.append(tile[:, : min(n - t * share, share) * slot_rows])
    spread = jnp.concatenate(tiles, axis=1) if len(tiles) > 1 else tiles[0]
    picked = dot(kernel, spread).astype(BF16)
    finish(recv_sem, 1, pack_in.at[rest, head])
    packed = pack_in[...].reshape(n * slot_rows, Q)
    overlap = dot(picked, packed)

    for j in range(n):
        sums_out[j, :, 0:C] = predicted[own * j : own * (j + 1)]
        sums_out[j, :, C : C + Q] = overlap[own * j : own * (j + 1)]
    sums_in[me] = sums_out[me]

    def send_sums(k):
        j = center_peer(k)
        send(sums_out.at[j], sums_in.at[me], 3, {"center": j})

    def send_group(k):
        send(feat_all.at[mb], feat_all.at[mb], 4, {"batch": batch_peer(k)})

    each(n - 1, send_sums)
    each(nb - 1, send_group)
    own_basis = dot(spread, packed).astype(BF16)
    labels_load.wait()
    targets = dot(pick, labels[...])[0:own]
    damping_load.wait()
    scale = damping_ref[...] * step_rate

    finish(recv_sem, 3, sums_in.at[rest])
    total = jnp.sum(sums_in[...], axis=0)
    residual = (total[:, 0:C] - targets).astype(BF16)
    out_r[...] = residual
    back[me, :, 0:C] = residual.astype(F32)
    back[me, :, C : C + Q] = total[:, C:] * scale

    def send_back(k):
        send(back.at[me], back.at[me], 5, {"center": center_peer(k)})

    each(n - 1, send_back)

    finish(recv_sem, 4, feat_all.at[rest_b])
    all_features = feat_all[...].reshape(nb * group, D)
    twice = jnp.concatenate([all_features, all_features], axis=0)
    kernel_all = laplace(twice, sq_centers, centers_t[...]).astype(BF16).astype(F32)
    gradient_t = jnp.transpose(step_rate * kernel_all)

    finish(recv_sem, 5, back.at[rest])
    for j in range(n):
        back_f32[own * j : own * (j + 1), :] = back[j]
    overlap_f32 = back_f32[:, C : C + Q]
    overlap_high = overlap_f32.astype(BF16)
    back_all[mb, :, 0:C] = back_f32[:, 0:C].astype(BF16)
    back_all[mb, :, C : C + Q] = overlap_high
    back_all[mb, :, C + Q : C + 2 * Q] = (overlap_f32 - overlap_high.astype(F32)).astype(BF16)

    def send_back_batch(k):
        send(back_all.at[mb], back_all.at[mb], 6, {"batch": batch_peer(k)})

    each(nb - 1, send_back_batch)
    finish(recv_sem, 6, back_all.at[rest_b])

    everything = back_all[...].reshape(nb * group, C + 2 * Q)
    residuals = everything[:, 0:C]
    high, low = everything[:, C : C + Q], everything[:, C + Q :]
    mix = dot(own_basis, jnp.concatenate([high, high], axis=0), 1, 1)
    mix = mix + dot(own_basis, jnp.concatenate([low, low], axis=0), 1, 1) - gradient_t
    mix_high = mix.astype(BF16).astype(F32)
    is_high = lax.broadcasted_iota(jnp.int32, mix.shape, 1) < nb * group
    mix = jnp.where(is_high, mix_high, mix - mix_high).astype(BF16)
    change = dot(mix, jnp.concatenate([residuals, residuals], axis=0))
    out_w[...] = (weights[...].astype(F32) + change).astype(BF16)

    finish(send_sem, 0, feat.at[rest])
    finish(send_sem, 1, pack_in.at[rest, head])
    finish(send_sem, 2, place_in.at[rest])
    finish(send_sem, 3, sums_in.at[rest])
    finish(send_sem, 4, feat_all.at[rest_b])
    finish(send_sem, 5, back.at[rest])
    finish(send_sem, 6, back_all.at[rest_b])


def solution(mesh):
    n, nb = mesh.shape["center"], mesh.shape["batch"]

    def per_device(centers, weights, subset_index, basis, damping, stored, labels, picks):
        (PC, D), C = centers.shape, weights.shape[1]
        S, Q = basis.shape
        SP = round_up(S, LANES)
        own, pool_rows = picks.shape[1], stored.shape[1]
        group = own * n
        capacity = max(1, 4 * S // n)
        rank_rows = round_up(capacity, 16)
        slot_rows = 16
        while slot_rows < rank_rows:
            slot_rows *= 2
        hbm = pl.BlockSpec(memory_space=pltpu.HBM)
        vmem = pl.BlockSpec(memory_space=pltpu.VMEM)
        new_weights, residual = pl.pallas_call(
            functools.partial(step_kernel, n, nb, rank_rows, slot_rows),
            out_shape=(
                jax.ShapeDtypeStruct((PC, C), BF16),
                jax.ShapeDtypeStruct((own, C), BF16),
            ),
            in_specs=[hbm] * 8,
            out_specs=(vmem, vmem),
            scratch_shapes=[
                pltpu.VMEM((PC, D), BF16),
                pltpu.VMEM((PC, C), BF16),
                pltpu.VMEM((SP, Q), BF16),
                pltpu.VMEM((pool_rows, D), BF16),
                pltpu.VMEM((pool_rows, C), BF16),
                pltpu.VMEM((1, S), jnp.int32),
                pltpu.VMEM((1, Q), F32),
                pltpu.VMEM((1, own), jnp.int32),
                pltpu.VMEM((1, SP), jnp.int32),
                pltpu.VMEM((D, PC), BF16),
                pltpu.VMEM((n, own, D), F32),
                pltpu.VMEM((group, D), F32),
                pltpu.VMEM((nb, group, D), BF16),
                pltpu.VMEM((n, rank_rows, Q), BF16),
                pltpu.VMEM((n, slot_rows, Q), BF16),
                pltpu.VMEM((n, 1, LANES), F32),
                pltpu.VMEM((n, 1, LANES), F32),
                pltpu.VMEM((n, own, C + Q), F32),
                pltpu.VMEM((n, own, C + Q), F32),
                pltpu.VMEM((n, own, C + Q), F32),
                pltpu.VMEM((group, C + Q), F32),
                pltpu.VMEM((nb, group, C + 2 * Q), BF16),
                pltpu.SemaphoreType.DMA((8,)),
                pltpu.SemaphoreType.DMA((7,)),
                pltpu.SemaphoreType.DMA((7,)),
            ],
            compiler_params=pltpu.CompilerParams(
                collective_id=0, has_side_effects=True, vmem_limit_bytes=60 * 1024 * 1024
            ),
        )(
            centers,
            weights,
            subset_index.reshape(1, S),
            basis,
            damping.reshape(1, Q),
            stored[0],
            labels[0],
            picks,
        )
        return new_weights, residual[None]

    return jax.shard_map(
        per_device,
        mesh=mesh,
        in_specs=(
            P("center", None),
            P("center", None),
            P("center"),
            P("center", None),
            P(),
            P("batch", "center", None),
            P("batch", "center", None),
            P("batch", "center"),
        ),
        out_specs=(P("center", None), P("batch", "center", None)),
        check_vma=False,
    )
```

time: 33 us -> 28.5 us (0.86)
  local copies, waits for them, and re-layouts: 6.52 us -> 2.45 us
    unnamed x18 -> x4, local copies, waits for them, and re-layouts: 6.52 us -> 2.45 us
where the time goes in v2:
time: 28.5 us; the launch traced here: 28.4 us
  Pallas kernels  25.3 us (89%)
  local copies, waits for them, and re-layouts  2.45 us (9%)
  between operations  0.65 us (2%)
    pallas_call x1, Pallas kernels, per_device(): pl.pallas_call(functools.partial(step_kernel, n, nb, rank_rows, slot_rows...  25.3 us
    unnamed x4, local copies, waits for them, and re-layouts  2.45 us

profile of v2, /device:TPU:0, one launch (start us, length us, event | category | flops | bytes accessed | tf_op | source)
XLA Modules:
  0.0 28.4 jit_solution(3970651328561871233)
XLA Ops:
  0.6 25.3 %shard_map.95 = (bf16[512,512]{1,0:T(8,128)(2,1)}, bf16[2,512]{1,0:T(2,128)(2,1)}) custom-call(bf16[512,384]{1,0:T(8,128)(2,1)} %centers_h.1, bf16[512,512]{1,0:T(8,128)(2,1)} %weights_h.1, s32[1,96]{1,0:T(1,128)} %bitcast.9, bf16[96,256]{1,0:T(8,128)(2,1)} %basis_h.1, f32[1,256]{1,0:T(1,128)} %bitcast.8, bf16[64,384]{1,0:T(8,128)(2,1)} %bitcast.6, ...), custom_call_target="tpu_custom_call" | custom-call | tf_op jit(solution)/shard_map/pallas_call | solution.py:298
  25.9 0.0 copy-start
  25.9 1.9 %copy.12 = bf16[512,512]{1,0:T(8,128)(2,1)} copy(bf16[512,512]{1,0:T(8,128)(2,1)} %get-tuple-element.8) | data formatting | bytes 1048576
  27.8 0.0 copy-done
  27.8 0.6 %copy.13 = bf16[1,2,512]{2,1,0:T(2,128)(2,1)} copy(bf16[1,2,512]{2,1,0:T(2,128)(2,1)S(1)} %bitcast.7) | data formatting | bytes 4096
Async XLA Ops:
  25.9 1.9 %copy-start = (bf16[2,512]{1,0:T(2,128)(2,1)S(1)}, bf16[2,512]{1,0:T(2,128)(2,1)}, u32[]{:S(2)}) copy-start(bf16[2,512]{1,0:T(2,128)(2,1)} %get-tuple-element.5) | copy-start | bytes 6148

commit v3 on v2

--- a/solution.py
+++ b/solution.py
@@ -298,8 +298,8 @@
         new_weights, residual = pl.pallas_call(
             functools.partial(step_kernel, n, nb, rank_rows, slot_rows),
             out_shape=(
-                jax.ShapeDtypeStruct((PC, C), BF16),
-                jax.ShapeDtypeStruct((own, C), BF16),
+                pltpu.VMEM((PC, C), BF16),
+                pltpu.VMEM((own, C), BF16),
             ),
             in_specs=[hbm] * 8,
             out_specs=(vmem, vmem),

time: 28.5 us -> 26.7 us (0.937)
  local copies, waits for them, and re-layouts: 2.45 us -> 1.37 us
  Pallas kernels: 25.3 us -> 24.5 us
    unnamed x4 -> x2, local copies, waits for them, and re-layouts: 2.45 us -> 1.37 us
    pallas_call x1, Pallas kernels: 25.3 us -> 24.5 us  [per_device(): pl.pallas_call(functools.partial(step_kernel, n, nb, rank_rows, slot_rows...]
where the time goes in v3:
time: 26.7 us; the launch traced here: 26.5 us
  Pallas kernels  24.5 us (92%)
  local copies, waits for them, and re-layouts  1.37 us (5%)
  between operations  0.64 us (2%)
    pallas_call x1, Pallas kernels, per_device(): pl.pallas_call(functools.partial(step_kernel, n, nb, rank_rows, slot_rows...  24.5 us
    unnamed x2, local copies, waits for them, and re-layouts  1.37 us

profile of v3, /device:TPU:0, one launch (start us, length us, event | category | flops | bytes accessed | tf_op | source)
XLA Modules:
  0.0 26.5 jit_solution(15079133664605858235)
XLA Ops:
  0.6 24.5 %shard_map.95 = (bf16[512,512]{1,0:T(8,128)(2,1)S(1)}, bf16[2,512]{1,0:T(2,128)(2,1)S(1)}) custom-call(bf16[512,384]{1,0:T(8,128)(2,1)} %centers_h.1, bf16[512,512]{1,0:T(8,128)(2,1)} %weights_h.1, s32[1,96]{1,0:T(1,128)} %bitcast.9, bf16[96,256]{1,0:T(8,128)(2,1)} %basis_h.1, f32[1,256]{1,0:T(1,128)} %bitcast.8, bf16[64,384]{1,0:T(8,128)(2,1)} %bitcast.7, ...), custom_call_target="tpu_custom_call" | custom-call | tf_op jit(solution)/shard_map/pallas_call | solution.py:298
  25.1 0.8 %copy.12 = bf16[512,512]{1,0:T(8,128)(2,1)} copy(bf16[512,512]{1,0:T(8,128)(2,1)S(1)} %get-tuple-element.6) | data formatting | bytes 1048576
  25.9 0.6 %copy.13 = bf16[1,2,512]{2,1,0:T(2,128)(2,1)} copy(bf16[1,2,512]{2,1,0:T(2,128)(2,1)S(1)} %bitcast.5) | data formatting | bytes 4096

commit v4 on v3

--- a/solution.py
+++ b/solution.py
@@ -50,6 +50,10 @@
     own, D = feat.shape[1:]
     PC, C = weights.shape
     S, Q = basis_h.shape
+    Qh = Q // 2
+    half = lax.rem(mb, 2)
+    pair = mb + 1 - 2 * half
+    columns = pl.ds(pl.multiple_of(half * Qh, Qh), Qh)
     SP = basis.shape[0]
     pool_rows = pool.shape[0]
     group = own * n
@@ -61,11 +65,11 @@
                 (picks_h, picks_ref),
                 (pool_h, pool),
                 (idx_h, idx_ref),
-                (basis_h, basis.at[pl.ds(0, S)]),
+                (basis_h.at[:, columns], basis.at[pl.ds(0, S)]),
                 (centers_h, centers),
                 (weights_h, weights),
                 (labels_h, labels),
-                (damping_h, damping_ref),
+                (damping_h.at[:, columns], damping_ref),
             ]
         )
     ]
@@ -92,10 +96,10 @@
 
     idx_row[...] = jnp.full(idx_row.shape, -1, jnp.int32)
     if SP > S:
-        basis[pl.ds(S, SP - S), :] = jnp.zeros((SP - S, Q), BF16)
+        basis[pl.ds(S, SP - S), :] = jnp.zeros((SP - S, Qh), BF16)
     if slot_rows > rank_rows:
-        pack_in[:, pl.ds(rank_rows, slot_rows - rank_rows), :] = jnp.zeros(
-            (n, slot_rows - rank_rows, Q), BF16
+        pack_in[half, :, pl.ds(rank_rows, slot_rows - rank_rows), :] = jnp.zeros(
+            (n, slot_rows - rank_rows, Qh), BF16
         )
 
     def send(src, dst, i, device):
@@ -168,14 +172,14 @@
     chosen = (lax.broadcasted_iota(jnp.int32, (n * rank_rows, SP), 0) + 1).astype(F32) == packed_row
     chosen = jnp.where(chosen, 1.0, 0.0).astype(BF16)
     basis_load.wait()
-    pack_out[...] = dot(chosen, basis[...]).astype(BF16).reshape(n, rank_rows, Q)
+    pack_out[...] = dot(chosen, basis[...]).astype(BF16).reshape(n, rank_rows, Qh)
 
     def send_pack(k):
         j = center_peer(k)
-        send(pack_out.at[j], pack_in.at[me, head], 1, {"center": j})
+        send(pack_out.at[j], pack_in.at[half, me, head], 1, {"center": j})
 
     each(n - 1, send_pack)
-    pack_in[me, pl.ds(0, rank_rows), :] = pack_out[me]
+    pack_in[half, me, pl.ds(0, rank_rows), :] = pack_out[me]
 
     centers_load.wait()
     centers_t[...] = jnp.transpose(centers[...])
@@ -187,9 +191,16 @@
         feat_f32[own * j : own * (j + 1), :] = feat[j]
     group_features = feat_f32[...].astype(BF16)
     feat_all[mb] = group_features
+    send(feat_all.at[mb], feat_all.at[mb], 7, {"batch": pair})
     kernel = laplace(group_features, sq_centers, centers_t[...]).astype(BF16)
     weights_load.wait()
     predicted = dot(kernel, weights[...])
+
+    def send_group(k):
+        other = lax.rem(mb - half + 2 + k, nb)
+        send(feat_all.at[mb], feat_all.at[mb], 4, {"batch": other})
+
+    each(nb - 2, send_group)
 
     finish(recv_sem, 2, place_in.at[rest])
     tiles = []
@@ -201,30 +212,30 @@
         tile = jnp.where(local_row == row, 1.0, 0.0).astype(BF16)
         tiles.append(tile[:, : min(n - t * share, share) * slot_rows])
     spread = jnp.concatenate(tiles, axis=1) if len(tiles) > 1 else tiles[0]
-    picked = dot(kernel, spread).astype(BF16)
-    finish(recv_sem, 1, pack_in.at[rest, head])
-    packed = pack_in[...].reshape(n * slot_rows, Q)
+    finish(recv_sem, 7, feat_all.at[0])
+    pair_kernel = laplace(feat_all[pair], sq_centers, centers_t[...]).astype(BF16)
+    picked = dot(jnp.concatenate([kernel, pair_kernel], axis=0), spread).astype(BF16)
+    finish(recv_sem, 1, pack_in.at[0, rest, head])
+    packed = pack_in[half].reshape(n * slot_rows, Qh)
     overlap = dot(picked, packed)
 
     for j in range(n):
         sums_out[j, :, 0:C] = predicted[own * j : own * (j + 1)]
-        sums_out[j, :, C : C + Q] = overlap[own * j : own * (j + 1)]
+        sums_out[j, :, C : C + Qh] = overlap[own * j : own * (j + 1)]
+        sums_out[j, :, C + Qh :] = overlap[group + own * j : group + own * (j + 1)]
     sums_in[me] = sums_out[me]
 
     def send_sums(k):
         j = center_peer(k)
         send(sums_out.at[j], sums_in.at[me], 3, {"center": j})
 
-    def send_group(k):
-        send(feat_all.at[mb], feat_all.at[mb], 4, {"batch": batch_peer(k)})
-
     each(n - 1, send_sums)
-    each(nb - 1, send_group)
-    own_basis = dot(spread, packed).astype(BF16)
+    send(pack_in.at[half], pack_in.at[half], 8, {"batch": pair})
     labels_load.wait()
     targets = dot(pick, labels[...])[0:own]
     damping_load.wait()
     scale = damping_ref[...] * step_rate
+    scale = jnp.concatenate([scale, scale], axis=1)
 
     finish(recv_sem, 3, sums_in.at[rest])
     total = jnp.sum(sums_in[...], axis=0)
@@ -238,7 +249,11 @@
 
     each(n - 1, send_back)
 
-    finish(recv_sem, 4, feat_all.at[rest_b])
+    finish(recv_sem, 8, pack_in.at[0])
+    own_basis = jnp.concatenate(
+        [dot(spread, pack_in[q].reshape(n * slot_rows, Qh)).astype(BF16) for q in range(2)], axis=1
+    )
+    finish(recv_sem, 4, feat_all.at[pl.ds(0, nb - 2)])
     all_features = feat_all[...].reshape(nb * group, D)
     twice = jnp.concatenate([all_features, all_features], axis=0)
     kernel_all = laplace(twice, sq_centers, centers_t[...]).astype(BF16).astype(F32)
@@ -259,9 +274,19 @@
     each(nb - 1, send_back_batch)
     finish(recv_sem, 6, back_all.at[rest_b])
 
-    everything = back_all[...].reshape(nb * group, C + 2 * Q)
-    residuals = everything[:, 0:C]
-    high, low = everything[:, C : C + Q], everything[:, C + Q :]
+    residuals = back_all[:, :, 0:C].reshape(nb * group, C)
+
+    def overlap_part(start):
+        rows = []
+        for g in range(nb):
+            halves = []
+            for q in range(2):
+                at = start + (0 if q == g % 2 else Qh)
+                halves.append(back_all[g - g % 2 + q, :, at : at + Qh])
+            rows.append(jnp.concatenate(halves, axis=1))
+        return jnp.concatenate(rows, axis=0)
+
+    high, low = overlap_part(C), overlap_part(C + Q)
     mix = dot(own_basis, jnp.concatenate([high, high], axis=0), 1, 1)
     mix = mix + dot(own_basis, jnp.concatenate([low, low], axis=0), 1, 1) - gradient_t
     mix_high = mix.astype(BF16).astype(F32)
@@ -271,10 +296,12 @@
     out_w[...] = (weights[...].astype(F32) + change).astype(BF16)
 
     finish(send_sem, 0, feat.at[rest])
-    finish(send_sem, 1, pack_in.at[rest, head])
+    finish(send_sem, 1, pack_in.at[0, rest, head])
     finish(send_sem, 2, place_in.at[rest])
     finish(send_sem, 3, sums_in.at[rest])
-    finish(send_sem, 4, feat_all.at[rest_b])
+    finish(send_sem, 4, feat_all.at[pl.ds(0, nb - 2)])
+    finish(send_sem, 7, feat_all.at[0])
+    finish(send_sem, 8, pack_in.at[0])
     finish(send_sem, 5, back.at[rest])
     finish(send_sem, 6, back_all.at[rest_b])
 
@@ -306,19 +333,19 @@
             scratch_shapes=[
                 pltpu.VMEM((PC, D), BF16),
                 pltpu.VMEM((PC, C), BF16),
-                pltpu.VMEM((SP, Q), BF16),
+                pltpu.VMEM((SP, Q // 2), BF16),
                 pltpu.VMEM((pool_rows, D), BF16),
                 pltpu.VMEM((pool_rows, C), BF16),
                 pltpu.VMEM((1, S), jnp.int32),
-                pltpu.VMEM((1, Q), F32),
+                pltpu.VMEM((1, Q // 2), F32),
                 pltpu.VMEM((1, own), jnp.int32),
                 pltpu.VMEM((1, SP), jnp.int32),
                 pltpu.VMEM((D, PC), BF16),
                 pltpu.VMEM((n, own, D), F32),
                 pltpu.VMEM((group, D), F32),
                 pltpu.VMEM((nb, group, D), BF16),
-                pltpu.VMEM((n, rank_rows, Q), BF16),
-                pltpu.VMEM((n, slot_rows, Q), BF16),
+                pltpu.VMEM((n, rank_rows, Q // 2), BF16),
+                pltpu.VMEM((2, n, slot_rows, Q // 2), BF16),
                 pltpu.VMEM((n, 1, LANES), F32),
                 pltpu.VMEM((n, 1, LANES), F32),
                 pltpu.VMEM((n, own, C + Q), F32),
@@ -327,8 +354,8 @@
                 pltpu.VMEM((group, C + Q), F32),
                 pltpu.VMEM((nb, group, C + 2 * Q), BF16),
                 pltpu.SemaphoreType.DMA((8,)),
-                pltpu.SemaphoreType.DMA((7,)),
-                pltpu.SemaphoreType.DMA((7,)),
+                pltpu.SemaphoreType.DMA((9,)),
+                pltpu.SemaphoreType.DMA((9,)),
             ],
             compiler_params=pltpu.CompilerParams(
                 collective_id=0, has_side_effects=True, vmem_limit_bytes=60 * 1024 * 1024

time: 26.7 us -> 25 us (0.936)
  Pallas kernels: 24.5 us -> 22.8 us
    pallas_call x1, Pallas kernels: 24.5 us -> 22.8 us  [per_device(): pl.pallas_call(functools.partial(step_kernel, n, nb, rank_rows, slot_rows...]
where the time goes in v4:
time: 25 us; the launch traced here: 24.8 us
  Pallas kernels  22.8 us (91%)
  local copies, waits for them, and re-layouts  1.37 us (5%)
  between operations  0.64 us (3%)
    pallas_call x1, Pallas kernels, per_device(): pl.pallas_call(functools.partial(step_kernel, n, nb, rank_rows, slot_rows...  22.8 us
    unnamed x2, local copies, waits for them, and re-layouts  1.37 us

profile of v4, /device:TPU:0, one launch (start us, length us, event | category | flops | bytes accessed | tf_op | source)
XLA Modules:
  0.0 24.8 jit_solution(6999682996205541117)
XLA Ops:
  0.6 22.8 %shard_map.95 = (bf16[512,512]{1,0:T(8,128)(2,1)S(1)}, bf16[2,512]{1,0:T(2,128)(2,1)S(1)}) custom-call(bf16[512,384]{1,0:T(8,128)(2,1)} %centers_h.1, bf16[512,512]{1,0:T(8,128)(2,1)} %weights_h.1, s32[1,96]{1,0:T(1,128)} %bitcast.9, bf16[96,256]{1,0:T(8,128)(2,1)} %basis_h.1, f32[1,256]{1,0:T(1,128)} %bitcast.8, bf16[64,384]{1,0:T(8,128)(2,1)} %bitcast.7, ...), custom_call_target="tpu_custom_call" | custom-call | tf_op jit(solution)/shard_map/pallas_call | solution.py:325
  23.4 0.8 %copy.12 = bf16[512,512]{1,0:T(8,128)(2,1)} copy(bf16[512,512]{1,0:T(8,128)(2,1)S(1)} %get-tuple-element.6) | data formatting | bytes 1048576
  24.2 0.6 %copy.13 = bf16[1,2,512]{2,1,0:T(2,128)(2,1)} copy(bf16[1,2,512]{2,1,0:T(2,128)(2,1)S(1)} %bitcast.5) | data formatting | bytes 4096
